TPU v7x, 32 devices: a whole 2x2x4 slice. The times are simulated.
32 devices in a mesh: rows: 16 (over z, y, x), heads: 2 (over core).
Axes of the slice: x: 2, y: 2, z: 4, core: 2. Of those that a mesh axis runs over, the one named last changes fastest.
Arguments:
- dec_input: bfloat16 [24576, 512], P('rows'), may hold values from -6 to 6
- enc_output: bfloat16 [24576, 512], P('rows'), may hold values from -6 to 6
- dec_lengths: int32 [16, 16], P('rows'), may hold values from 1 to 768, 1536 in all within a row
- enc_lengths: int32 [16, 16], P('rows'), may hold values from 1 to 768, 1536 in all within a row
- w_self_qkv: bfloat16 [3, 512, 512], P(None, None, 'heads'), may hold values from -0.25 to 0.25
- w_self_out: bfloat16 [512, 512], P('heads'), may hold values from -1 to 1
- w_cross_q: bfloat16 [512, 512], P(None, 'heads'), may hold values from -0.25 to 0.25
- w_cross_kv: bfloat16 [2, 512, 512], P(None, None, 'heads'), may hold values from -0.25 to 0.25
- w_cross_out: bfloat16 [512, 512], P('heads'), may hold values from -1 to 1
- w_ffn_in: bfloat16 [512, 2048], P(None, 'heads'), may hold values from -0.25 to 0.25
- w_ffn_out: bfloat16 [2048, 512], P('heads'), may hold values from -0.125 to 0.125
- norm_gain: float32 [3, 512], replicated, may hold values from 0.25 to 1.75
- norm_bias: float32 [3, 512], replicated, may hold values from -1.75 to 1.75
- out_grad: bfloat16 [24576, 512], P('rows'), may hold values from -6 to 6
Outputs:
- layer_out: float32 [24576, 512], P(('rows', 'heads'))
- input_grad: float32 [24576, 512], P(('rows', 'heads'))
- enc_grad: float32 [24576, 512], P(('rows', 'heads'))
- grad_self_qkv: float32 [3, 512, 512], P(None, None, 'heads')
- grad_self_out: float32 [512, 512], P('heads')
- grad_cross_q: float32 [512, 512], P(None, 'heads')
- grad_cross_kv: float32 [2, 512, 512], P(None, None, 'heads')
- grad_cross_out: float32 [512, 512], P('heads')
- grad_ffn_in: float32 [512, 2048], P(None, 'heads')
- grad_ffn_out: float32 [2048, 512], P('heads')
- grad_norm_gain: float32 [3, 512], replicated
- grad_norm_bias: float32 [3, 512], replicated
Inputs may be any that keep to these rules, and one draw needn't show every extreme that they name: `dec_lengths`: in every row the 16 lengths sum to 1536 and the largest is exactly 768. `enc_lengths`: in every row the 16 lengths sum to 1536 and the largest is exactly 768.
All inputs are finite; a program needn't handle non-finite values.
Results may differ from a plain program's by a relative error of at most 0.025.
The roundings to bfloat16 on the way count: a program that leaves them out, or rounds other values in their place, can miss the bound.
Values may be sent and summed in bfloat16 or wider, within the bound.
A program may use at most 256 MiB of HBM per device.

v0:
```python
import functools

import jax
import jax.numpy as jnp
from jax import lax
from jax.experimental import pallas as pl
from jax.experimental.pallas import tpu as pltpu
from jax.sharding import PartitionSpec as P

HEAD_DIM = 64
LANES = 128
SPAN = 256
NORM_EPS = 1e-05
MASKED_SCORE = -1e30
LOG2_E = 1.4426950408889634
GELU_RATE = 0.7978845608028654
GELU_CUBE = 0.044715
F32 = jnp.float32
BF16 = jnp.bfloat16
NT = (((1,), (1,)), ((), ()))
TN = (((0,), (0,)), ((), ()))
VMEM = pl.BlockSpec(memory_space=pltpu.VMEM)
SMEM = pl.BlockSpec(memory_space=pltpu.SMEM)


def dot(left, right):
    return jnp.dot(left, right, preferred_element_type=F32)


def dot_nt(left, right):
    return lax.dot_general(left, right, NT, preferred_element_type=F32)


def dot_tn(left, right):
    return lax.dot_general(left, right, TN, preferred_element_type=F32)


def shape_of(dims, kind):
    return jax.ShapeDtypeStruct(dims, kind)


def call(kernel, outs, scratch, mib, *args, smem=0):
    return pl.pallas_call(
        kernel,
        out_shape=outs,
        in_specs=[SMEM] * smem + [VMEM] * (len(args) - smem),
        out_specs=jax.tree.map(lambda _: VMEM, outs),
        scratch_shapes=scratch,
        compiler_params=pltpu.CompilerParams(vmem_limit_bytes=mib * 2**20),
    )(*args)


def segment_bounds(len_ref):
    starts, ends, total = [], [], jnp.int32(0)
    for k in range(len_ref.shape[1]):
        starts.append(total)
        total = total + len_ref[0, k]
        ends.append(total)
    return starts, ends


def bound_lanes(starts, ends):
    lane = lax.broadcasted_iota(jnp.int32, (1, LANES), 1)
    first = jnp.full((1, LANES), 1 << 30, jnp.int32)
    last = jnp.zeros((1, LANES), jnp.int32)
    for k, (start, end) in enumerate(zip(starts, ends)):
        first = jnp.where(lane == HEAD_DIM + k, start, first)
        last = jnp.where(lane == HEAD_DIM + k, end, last)
    return first, last


def lanes_of(rows):
    return lax.broadcasted_iota(jnp.int32, (rows, LANES), 1)


def membership(first_row, rows, bounds):
    place = lax.broadcasted_iota(jnp.int32, (rows, LANES), 0) + first_row
    return (place >= bounds[0]) & (place < bounds[1])


def query_extra(first_row, rows, bounds):
    return jnp.where(membership(first_row, rows, bounds), F32(MASKED_SCORE), F32(0.0))


def key_extra(first_row, rows, bounds, segs):
    lane = lanes_of(rows)
    used = (lane >= HEAD_DIM) & (lane < HEAD_DIM + segs + 3)
    return jnp.where(used & ~membership(first_row, rows, bounds), F32(1.0), F32(0.0))


def value_extra(rows):
    lane = lanes_of(rows)
    return jnp.where((lane >= HEAD_DIM) & (lane < HEAD_DIM + 2), F32(1.0), F32(0.0))


def head_slab(wide, head):
    if wide.shape[1] < LANES:
        return jnp.concatenate([wide, jnp.zeros_like(wide)], axis=1)
    first = head // 2 * LANES
    slab = wide[:, first : first + LANES]
    if head % 2:
        slab = pltpu.roll(slab, HEAD_DIM, 1)
    return slab


def put_heads(dest, where, wide, extra):
    low_lanes = lanes_of(wide.shape[0]) < HEAD_DIM
    for head in range(dest.shape[0]):
        dest[head, where, :] = jnp.where(low_lanes, head_slab(wide, head), extra).astype(dest.dtype)


def join_heads(dest, where, slabs):
    if len(slabs) == 1:
        dest[where, :] = slabs[0][:, :HEAD_DIM].astype(dest.dtype)
        return
    low_lanes = lanes_of(slabs[0].shape[0]) < HEAD_DIM
    for pair in range(len(slabs) // 2):
        both = jnp.where(low_lanes, slabs[2 * pair], pltpu.roll(slabs[2 * pair + 1], HEAD_DIM, 1))
        dest[where, pair * LANES : (pair + 1) * LANES] = both.astype(dest.dtype)


def span_for(block, length, from_starts, to_starts, to_ends):
    first_row = block * SPAN
    last_row = first_row + SPAN - 1
    low, high = jnp.int32(0), jnp.int32(0)
    for start, to_start, to_end in zip(from_starts, to_starts, to_ends):
        low = jnp.where(start <= first_row, to_start, low)
        high = jnp.where(start <= last_row, to_end, high)
    low = (low >> 7) << 7
    pieces = (high - low + SPAN - 1) >> 8
    return jnp.minimum(low, length - pieces * SPAN), pieces


def each_span(length, starts_from, starts_to, ends_to, body):
    def step(block, carry):
        start, pieces = span_for(block, length, starts_from, starts_to, ends_to)
        start = pl.multiple_of(start, LANES)
        rows = pl.ds(pl.multiple_of(block * SPAN, SPAN), SPAN)
        for count in range(1, length // SPAN + 1):

            @pl.when(pieces == count)
            def _():
                body(rows, pl.ds(start, count * SPAN))

        return carry

    lax.fori_loop(0, length // SPAN, step, 0)


def attend_body(qx, kx, vx, ctx, segs, rows, keys):
    scale = LOG2_E * HEAD_DIM**-0.5
    lane = lanes_of(SPAN)
    slabs = []
    for head in range(qx.shape[0]):
        query = qx[head, rows, :]
        scores = dot_nt(query, kx[head, keys, :])
        peak = jnp.max(scores, axis=1, keepdims=True)
        raised = jnp.exp2((scores - peak) * scale).astype(BF16)
        mixed = dot(raised, vx[head, keys, :])
        total = mixed[:, HEAD_DIM : HEAD_DIM + 1]
        slabs.append(mixed / total)
        level = -(peak + jnp.log(total) * (HEAD_DIM**0.5))
        high = level.astype(BF16).astype(F32)
        middle = (level - high).astype(BF16).astype(F32)
        low = level - high - middle
        base = HEAD_DIM + segs
        wide = query.astype(F32)
        wide = jnp.where(lane == base, high, wide)
        wide = jnp.where(lane == base + 1, middle, wide)
        wide = jnp.where(lane == base + 2, low, wide)
        qx[head, rows, :] = wide.astype(BF16)
    join_heads(ctx, rows, slabs)


def split_out(source, keep, send, share):
    me = lax.axis_index("heads")
    parts = send.shape[0] + 1
    for k in range(parts):
        owner = lax.rem(me + k, parts)
        rows = pl.ds(pl.multiple_of(owner * share, share), share)
        if k == 0:
            keep[...] = source[rows, :].astype(keep.dtype)
        else:
            send[k - 1] = source[rows, :].astype(send.dtype)


def self_forward_kernel(len_ref, x_ref, w_ref, keep, send, ctx, qx, kx, vx):
    length = x_ref.shape[0]
    segs = len_ref.shape[1]
    starts, ends = segment_bounds(len_ref)
    bounds = bound_lanes(starts, ends)

    def project(block, carry):
        first = pl.multiple_of(block * SPAN, SPAN)
        rows = pl.ds(first, SPAN)
        tokens = x_ref[rows, :]
        put_heads(qx, rows, dot(tokens, w_ref[0]), query_extra(first, SPAN, bounds))
        put_heads(kx, rows, dot(tokens, w_ref[1]), key_extra(first, SPAN, bounds, segs))
        put_heads(vx, rows, dot(tokens, w_ref[2]), value_extra(SPAN))
        return carry

    lax.fori_loop(0, length // SPAN, project, 0)
    each_span(
        length, starts, starts, ends, functools.partial(attend_body, qx, kx, vx, ctx, segs)
    )
    split_out(ctx, keep, send, keep.shape[0])


def cross_keys_kernel(len_ref, x_ref, w_ref, kx, vx):
    length = x_ref.shape[0]
    bounds = bound_lanes(*segment_bounds(len_ref))
    segs = len_ref.shape[1]

    def project(block, carry):
        first = pl.multiple_of(block * SPAN, SPAN)
        rows = pl.ds(first, SPAN)
        tokens = x_ref[rows, :]
        put_heads(kx, rows, dot(tokens, w_ref[0]), key_extra(first, SPAN, bounds, segs))
        put_heads(vx, rows, dot(tokens, w_ref[1]), value_extra(SPAN))
        return carry

    lax.fori_loop(0, length // SPAN, project, 0)


def gather_rows(dest, own, others):
    me = lax.axis_index("heads")
    parts = len(others) + 1
    share = own.shape[0]
    for k, source in enumerate([own, *others]):
        owner = lax.rem(me + k, parts)
        dest[pl.ds(pl.multiple_of(owner * share, share), share), :] = source[...]


def cross_forward_kernel(parts, dec_ref, enc_ref, kx, vx, *refs):
    pieces, (keep, send, ctx, qx, flat) = refs[:parts], refs[parts:]
    length = ctx.shape[0]
    segs = dec_ref.shape[1]
    dec_starts, dec_ends = segment_bounds(dec_ref)
    enc_starts, enc_ends = segment_bounds(enc_ref)
    bounds = bound_lanes(dec_starts, dec_ends)
    gather_rows(flat, pieces[0], pieces[1:])

    def widen(block, carry):
        first = pl.multiple_of(block * SPAN, SPAN)
        rows = pl.ds(first, SPAN)
        put_heads(qx, rows, flat[rows, :].astype(F32), query_extra(first, SPAN, bounds))
        return carry

    lax.fori_loop(0, length // SPAN, widen, 0)
    each_span(
        length, dec_starts, enc_starts, enc_ends,
        functools.partial(attend_body, qx, kx, vx, ctx, segs),
    )
    split_out(ctx, keep, send, keep.shape[0])


def attend_back_body(qx, kx, vx, gx, dq, dk, dv, rows, queries):
    scale = LOG2_E * HEAD_DIM**-0.5
    key_slabs, value_slabs = [], []
    for head in range(qx.shape[0]):
        keys = kx[head, rows, :]
        query = qx[head, queries, :]
        grads = gx[head, queries, :]
        weights = jnp.exp2(dot_nt(keys, query) * scale)
        raised = dot_nt(vx[head, rows, :], grads)
        value_slabs.append(dot(weights.astype(BF16), grads))
        inner = (weights * raised).astype(BF16)
        key_slabs.append(dot(inner, query) * (HEAD_DIM**-0.5))
        dq[head, queries, :] += dot_tn(inner, keys)
    join_heads(dk, rows, key_slabs)
    join_heads(dv, rows, value_slabs)


def attend_back(key_starts, key_ends, query_starts, query_ends, qx, kx, vx, ctx, grad, gx, dq, sq, sk, sv):
    length = ctx.shape[0]
    heads = qx.shape[0]
    lane = lanes_of(SPAN)

    def widen(block, carry):
        rows = pl.ds(pl.multiple_of(block * SPAN, SPAN), SPAN)
        wide = grad[rows, :].astype(F32)
        product = wide * ctx[rows, :].astype(F32)
        for head in range(heads):
            slab = head_slab(product, head)
            level = -jnp.sum(jnp.where(lane < HEAD_DIM, slab, 0.0), axis=1, keepdims=True)
            high = level.astype(BF16).astype(F32)
            extra = jnp.where(lane == HEAD_DIM, high, 0.0)
            extra = jnp.where(lane == HEAD_DIM + 1, level - high, extra)
            full = jnp.where(lane < HEAD_DIM, head_slab(wide, head), extra)
            gx[head, rows, :] = full.astype(BF16)
            dq[head, rows, :] = jnp.zeros((SPAN, LANES), F32)
        return carry

    lax.fori_loop(0, length // SPAN, widen, 0)
    each_span(
        length, key_starts, query_starts, query_ends,
        functools.partial(attend_back_body, qx, kx, vx, gx, dq, sk, sv),
    )

    def finish(block, carry):
        rows = pl.ds(pl.multiple_of(block * SPAN, SPAN), SPAN)
        join_heads(sq, rows, [dq[head, rows, :] * (HEAD_DIM**-0.5) for head in range(heads)])
        return carry

    lax.fori_loop(0, length // SPAN, finish, 0)


def norm_forward(summed, gain, bias):
    center = summed - jnp.mean(summed, axis=1, keepdims=True)
    inverse_dev = lax.rsqrt(jnp.mean(center * center, axis=1, keepdims=True) + NORM_EPS)
    normed = center * inverse_dev
    return normed * gain + bias, normed, inverse_dev


def norm_back(grad, normed, inverse_dev, gain):
    scaled = grad * gain
    back = inverse_dev * (
        scaled
        - jnp.mean(scaled, axis=1, keepdims=True)
        - normed * jnp.mean(scaled * normed, axis=1, keepdims=True)
    )
    gain_grad = jnp.sum(grad * normed, axis=0, keepdims=True)
    return back, gain_grad, jnp.sum(grad, axis=0, keepdims=True)


def share_block(share):
    return 256 if share % 256 == 0 else share


def own_rows(share, first, rows):
    start = lax.axis_index("heads") * share + first
    return pl.ds(pl.multiple_of(start, 64), rows)


def first_norm_kernel(parts, x_ref, gain, bias, *refs):
    ctx, w_out, w_query = refs[:parts], refs[parts : 2 * parts], refs[2 * parts : 3 * parts]
    first_out, first_low, normed_out, dev_out, keep, send = refs[3 * parts :]
    share = first_out.shape[0]
    block = share_block(share)

    def step(index, carry):
        first = pl.multiple_of(index * block, block)
        rows = pl.ds(first, block)
        total = x_ref[own_rows(share, first, block), :].astype(F32)
        for k in range(parts):
            total = total + dot(ctx[k][rows, :], w_out[k][...])
        result, normed, inverse_dev = norm_forward(total, gain[0:1, :], bias[0:1, :])
        low = result.astype(BF16)
        first_out[rows, :] = result
        first_low[rows, :] = low
        normed_out[rows, :] = normed
        dev_out[rows, :] = inverse_dev
        for k in range(parts):
            value = dot(low, w_query[k][...]).astype(BF16)
            if k == 0:
                keep[rows, :] = value
            else:
                send[k - 1, rows, :] = value
        return carry

    lax.fori_loop(0, share // block, step, 0)


def middle_kernel(parts, gain, bias, first_out, out_grad, *refs):
    groups = [refs[g * parts : (g + 1) * parts] for g in range(4)]
    ctx, w_cross, w_in, w_out = groups
    (layer_out, grad_mid, gains, biases, g_out_keep, g_out_send, g_in_keep, g_in_send,
     g_cross_keep, g_cross_send, back_keep, back_send,
     second, second_low, normed2, dev2, total, hidden, slope, top_low, back_sum) = refs[4 * parts :]
    share = first_out.shape[0]
    block = share_block(share)
    units = w_in[0].shape[1]
    chunk = min(256, units)

    def enter(index, carry):
        rows = pl.ds(pl.multiple_of(index * block, block), block)
        summed = first_out[rows, :]
        for k in range(parts):
            summed = summed + dot(ctx[k][rows, :], w_cross[k][...])
        result, normed, inverse_dev = norm_forward(summed, gain[1:2, :], bias[1:2, :])
        second[rows, :] = result
        second_low[rows, :] = result.astype(BF16)
        normed2[rows, :] = normed
        dev2[rows, :] = inverse_dev
        return carry

    lax.fori_loop(0, share // block, enter, 0)
    total[...] = second[...]
    for k in range(parts):

        def expand(index, carry):
            cols = pl.ds(pl.multiple_of(index * chunk, chunk), chunk)
            spot = k * (units // chunk) + index
            pre = dot(second_low[...], w_in[k][:, cols])
            square = pre * pre
            bent = jnp.tanh(pre * (GELU_RATE + (GELU_RATE * GELU_CUBE) * square))
            half = 0.5 + 0.5 * bent
            act = (pre * half).astype(BF16)
            hidden[spot] = act
            bend = (0.5 - 0.5 * bent * bent) * (
                GELU_RATE + (3.0 * GELU_RATE * GELU_CUBE) * square
            )
            slope[spot] = half + pre * bend
            total[...] += dot(act, w_out[k][cols, :])
            return carry

        lax.fori_loop(0, units // chunk, expand, 0)

    gains[...] = jnp.zeros_like(gains)
    biases[...] = jnp.zeros_like(biases)

    def turn(index, carry):
        first = pl.multiple_of(index * block, block)
        rows = pl.ds(first, block)
        result, normed, inverse_dev = norm_forward(total[rows, :], gain[2:3, :], bias[2:3, :])
        layer_out[rows, :] = result
        grad = out_grad[own_rows(share, first, block), :].astype(F32)
        back, gain_grad, bias_grad = norm_back(grad, normed, inverse_dev, gain[2:3, :])
        gains[1:2, :] += gain_grad
        biases[1:2, :] += bias_grad
        back_sum[rows, :] = back
        top_low[rows, :] = back.astype(BF16)
        return carry

    lax.fori_loop(0, share // block, turn, 0)
    for k in range(parts):

        def contract(index, carry):
            cols = pl.ds(pl.multiple_of(index * chunk, chunk), chunk)
            spot = k * (units // chunk) + index
            weight_out = dot_tn(hidden[spot], top_low[...]).astype(BF16)
            pre = (dot_nt(top_low[...], w_out[k][cols, :]) * slope[spot]).astype(BF16)
            weight_in = dot_tn(second_low[...], pre).astype(BF16)
            if k == 0:
                g_out_keep[cols, :] = weight_out
                g_in_keep[:, cols] = weight_in
            else:
                g_out_send[k - 1, cols, :] = weight_out
                g_in_send[k - 1, :, cols] = weight_in
            back_sum[...] += dot_nt(pre, w_in[k][:, cols])
            return carry

        lax.fori_loop(0, units // chunk, contract, 0)

    def leave(index, carry):
        rows = pl.ds(pl.multiple_of(index * block, block), block)
        back, gain_grad, bias_grad = norm_back(
            back_sum[rows, :], normed2[rows, :], dev2[rows, :], gain[1:2, :]
        )
        gains[0:1, :] += gain_grad
        biases[0:1, :] += bias_grad
        grad_mid[rows, :] = back
        low = back.astype(BF16)
        top_low[rows, :] = low
        for k in range(parts):
            value = dot_nt(low, w_cross[k][...]).astype(BF16)
            if k == 0:
                back_keep[rows, :] = value
            else:
                back_send[k - 1, rows, :] = value
        return carry

    lax.fori_loop(0, share // block, leave, 0)
    for k in range(parts):
        value = dot_tn(ctx[k][...], top_low[...]).astype(BF16)
        if k == 0:
            g_cross_keep[...] = value
        else:
            g_cross_send[k - 1] = value


def cross_back_kernel(parts, dec_ref, enc_ref, qx, kx, vx, ctx, enc, w_kv, *refs):
    pieces = refs[:parts]
    (gq_keep, gq_send, g_kv, enc_keep, enc_send, grad, gx, dq, sq, sk, sv, wide) = refs[parts:]
    length = ctx.shape[0]
    dec_starts, dec_ends = segment_bounds(dec_ref)
    enc_starts, enc_ends = segment_bounds(enc_ref)
    gather_rows(grad, pieces[0], pieces[1:])
    attend_back(
        enc_starts, enc_ends, dec_starts, dec_ends, qx, kx, vx, ctx, grad, gx, dq, sq, sk, sv
    )
    split_out(sq, gq_keep, gq_send, gq_keep.shape[0])
    g_kv[0] = dot_tn(enc[...], sk[...]).astype(BF16)
    g_kv[1] = dot_tn(enc[...], sv[...]).astype(BF16)

    def step(block, carry):
        rows = pl.ds(pl.multiple_of(block * SPAN, SPAN), SPAN)
        wide[rows, :] = dot_nt(sk[rows, :], w_kv[0]) + dot_nt(sv[rows, :], w_kv[1])
        return carry

    lax.fori_loop(0, length // SPAN, step, 0)
    split_out(wide, enc_keep, enc_send, enc_keep.shape[0])


def first_back_kernel(parts, gain, grad_mid, first_low, normed, dev, *refs):
    groups = [refs[g * parts : (g + 1) * parts] for g in range(4)]
    gq, w_query, ctx, w_out = groups
    (grad_base, gains, biases, g_query_keep, g_query_send, g_out_keep, g_out_send,
     back_keep, back_send, low_ref) = refs[4 * parts :]
    share = grad_mid.shape[0]
    block = share_block(share)
    gains[...] = jnp.zeros_like(gains)
    biases[...] = jnp.zeros_like(biases)

    def step(index, carry):
        rows = pl.ds(pl.multiple_of(index * block, block), block)
        grad = grad_mid[rows, :]
        for k in range(parts):
            grad = grad + dot_nt(gq[k][rows, :], w_query[k][...])
        back, gain_grad, bias_grad = norm_back(grad, normed[rows, :], dev[rows, :], gain[0:1, :])
        gains[...] += gain_grad
        biases[...] += bias_grad
        grad_base[rows, :] = back
        low = back.astype(BF16)
        low_ref[rows, :] = low
        for k in range(parts):
            value = dot_nt(low, w_out[k][...]).astype(BF16)
            if k == 0:
                back_keep[rows, :] = value
            else:
                back_send[k - 1, rows, :] = value
        return carry

    lax.fori_loop(0, share // block, step, 0)
    for k in range(parts):
        query_grad = dot_tn(first_low[...], gq[k][...]).astype(BF16)
        out_grad = dot_tn(ctx[k][...], low_ref[...]).astype(BF16)
        if k == 0:
            g_query_keep[...] = query_grad
            g_out_keep[...] = out_grad
        else:
            g_query_send[k - 1] = query_grad
            g_out_send[k - 1] = out_grad


def self_back_kernel(parts, dec_ref, qx, kx, vx, ctx, x_ref, w_qkv, *refs):
    pieces = refs[:parts]
    g_qkv, in_keep, in_send, grad, gx, dq, sq, sk, sv, wide = refs[parts:]
    length = ctx.shape[0]
    starts, ends = segment_bounds(dec_ref)
    gather_rows(grad, pieces[0], pieces[1:])
    attend_back(starts, ends, starts, ends, qx, kx, vx, ctx, grad, gx, dq, sq, sk, sv)
    for c, source in enumerate((sq, sk, sv)):
        g_qkv[c] = dot_tn(x_ref[...], source[...]).astype(BF16)

    def step(block, carry):
        rows = pl.ds(pl.multiple_of(block * SPAN, SPAN), SPAN)
        wide[rows, :] = (
            dot_nt(sq[rows, :], w_qkv[0])
            + dot_nt(sk[rows, :], w_qkv[1])
            + dot_nt(sv[rows, :], w_qkv[2])
        )
        return carry

    lax.fori_loop(0, length // SPAN, step, 0)
    split_out(wide, in_keep, in_send, in_keep.shape[0])


def body(
    dec_input,
    enc_output,
    dec_lengths,
    enc_lengths,
    w_self_qkv,
    w_self_out,
    w_cross_q,
    w_cross_kv,
    w_cross_out,
    w_ffn_in,
    w_ffn_out,
    norm_gain,
    norm_bias,
    out_grad,
):
    parts = lax.axis_size("heads")
    length, width = dec_input.shape
    local = w_self_out.shape[0]
    heads = local // HEAD_DIM
    share = length // parts
    units = w_ffn_in.shape[1]
    chunk = min(256, units)
    chunks = parts * units // chunk

    def shift(value, k):
        return lax.ppermute(value, "heads", [(d, (d + k) % parts) for d in range(parts)])

    def slots(shard):
        return [shard] + [shift(shard, parts - k) for k in range(1, parts)]

    def swap(keep, send):
        return [keep] + [shift(send[parts - k - 1], parts - k) for k in range(1, parts)]

    def collect(keep, send):
        total = keep.astype(F32)
        for k in range(1, parts):
            total = total + shift(send[k - 1], k).astype(F32)
        return total

    self_out, cross_q, cross_out = slots(w_self_out), slots(w_cross_q), slots(w_cross_out)
    ffn_in, ffn_out = slots(w_ffn_in), slots(w_ffn_out)

    def sent(*dims, kind=BF16):
        return shape_of((parts - 1, *dims), kind)

    def own(*dims, kind=BF16):
        return shape_of(dims, kind)

    wide_heads = own(heads, length, LANES)
    self_keep, self_send, self_ctx, self_qx, self_kx, self_vx = call(
        self_forward_kernel,
        [own(share, local), sent(share, local), own(length, local), wide_heads, wide_heads, wide_heads],
        [], 40, dec_lengths, dec_input, w_self_qkv, smem=1,
    )
    self_slots = swap(self_keep, self_send)
    cross_kx, cross_vx = call(
        cross_keys_kernel, [wide_heads, wide_heads], [], 32,
        enc_lengths, enc_output, w_cross_kv, smem=1,
    )
    first_out, first_low, first_normed, first_dev, query_keep, query_send = call(
        functools.partial(first_norm_kernel, parts),
        [own(share, width, kind=F32), own(share, width), own(share, width, kind=F32),
         own(share, 1, kind=F32), own(share, local), sent(share, local)],
        [], 32, dec_input, norm_gain, norm_bias, *self_slots, *self_out, *cross_q,
    )
    cross_keep, cross_send, cross_ctx, cross_qx = call(
        functools.partial(cross_forward_kernel, parts),
        [own(share, local), sent(share, local), own(length, local), wide_heads],
        [pltpu.VMEM((length, local), BF16)], 40,
        dec_lengths, enc_lengths, cross_kx, cross_vx, *swap(query_keep, query_send), smem=2,
    )
    cross_slots = swap(cross_keep, cross_send)
    (layer_out, grad_mid, gains_high, biases_high, g_ffn_out, g_ffn_out_send, g_ffn_in,
     g_ffn_in_send, g_cross_out, g_cross_out_send, back_keep, back_send) = call(
        functools.partial(middle_kernel, parts),
        [own(share, width, kind=F32), own(share, width, kind=F32),
         own(2, width, kind=F32), own(2, width, kind=F32),
         own(units, width), sent(units, width), own(width, units), sent(width, units),
         own(local, width), sent(local, width), own(share, local), sent(share, local)],
        [pltpu.VMEM((share, width), F32), pltpu.VMEM((share, width), BF16),
         pltpu.VMEM((share, width), F32), pltpu.VMEM((share, 1), F32),
         pltpu.VMEM((share, width), F32), pltpu.VMEM((chunks, share, chunk), BF16),
         pltpu.VMEM((chunks, share, chunk), F32), pltpu.VMEM((share, width), BF16),
         pltpu.VMEM((share, width), F32)],
        56, norm_gain, norm_bias, first_out, out_grad,
        *cross_slots, *cross_out, *ffn_in, *ffn_out,
    )
    back_scratch = [
        pltpu.VMEM((length, local), BF16),
        pltpu.VMEM((heads, length, LANES), BF16),
        pltpu.VMEM((heads, length, LANES), F32),
        pltpu.VMEM((length, local), BF16),
        pltpu.VMEM((length, local), BF16),
        pltpu.VMEM((length, local), BF16),
        pltpu.VMEM((length, width), F32),
    ]
    gq_keep, gq_send, g_cross_kv, enc_keep, enc_send = call(
        functools.partial(cross_back_kernel, parts),
        [own(share, local), sent(share, local), own(2, width, local),
         own(share, width, kind=F32), sent(share, width)],
        back_scratch, 56, dec_lengths, enc_lengths, cross_qx, cross_kx, cross_vx, cross_ctx,
        enc_output, w_cross_kv, *swap(back_keep, back_send), smem=2,
    )
    enc_grad = collect(enc_keep, enc_send)
    (grad_base, gains_low, biases_low, g_cross_q, g_cross_q_send, g_self_out, g_self_out_send,
     self_back_keep, self_back_send) = call(
        functools.partial(first_back_kernel, parts),
        [own(share, width, kind=F32), own(1, width, kind=F32), own(1, width, kind=F32),
         own(width, local), sent(width, local), own(local, width), sent(local, width),
         own(share, local), sent(share, local)],
        [pltpu.VMEM((share, width), BF16)], 40,
        norm_gain, grad_mid, first_low, first_normed, first_dev,
        *swap(gq_keep, gq_send), *cross_q, *self_slots, *self_out,
    )
    g_self_qkv, in_keep, in_send = call(
        functools.partial(self_back_kernel, parts),
        [own(3, width, local), own(share, width, kind=F32), sent(share, width)],
        back_scratch, 56, dec_lengths, self_qx, self_kx, self_vx, self_ctx, dec_input,
        w_self_qkv, *swap(self_back_keep, self_back_send), smem=1,
    )
    input_grad = grad_base + collect(in_keep, in_send)

    def over_rows(value):
        return lax.psum(value.astype(BF16), "rows").astype(F32)

    return (
        layer_out,
        input_grad,
        enc_grad,
        over_rows(g_self_qkv),
        over_rows(collect(g_self_out, g_self_out_send)),
        over_rows(collect(g_cross_q, g_cross_q_send)),
        over_rows(g_cross_kv),
        over_rows(collect(g_cross_out, g_cross_out_send)),
        over_rows(collect(g_ffn_in, g_ffn_in_send)),
        over_rows(collect(g_ffn_out, g_ffn_out_send)),
        lax.psum(jnp.concatenate([gains_low, gains_high]), ("rows", "heads")),
        lax.psum(jnp.concatenate([biases_low, biases_high]), ("rows", "heads")),
    )


def solution(mesh):
    in_specs = (
        P("rows", None),
        P("rows", None),
        P("rows", None),
        P("rows", None),
        P(None, None, "heads"),
        P("heads", None),
        P(None, "heads"),
        P(None, None, "heads"),
        P("heads", None),
        P(None, "heads"),
        P("heads", None),
        P(),
        P(),
        P("rows", None),
    )
    out_specs = (
        P(("rows", "heads"), None),
        P(("rows", "heads"), None),
        P(("rows", "heads"), None),
        P(None, None, "heads"),
        P("heads", None),
        P(None, "heads"),
        P(None, None, "heads"),
        P("heads", None),
        P(None, "heads"),
        P("heads", None),
        P(),
        P(),
    )
    return jax.shard_map(body, mesh=mesh, in_specs=in_specs, out_specs=out_specs, check_vma=False)
```

profile of v0, /device:TPU:0, one launch (start us, length us, event | category | flops | bytes accessed | tf_op | source)
XLA Modules:
  0.0 364.8 jit_solution(13222774066773773304)
XLA Ops:
  7.2 1.4 copy-done
  10.4 15.5 %shard_map.229 = (bf16[768,256]{1,0:T(8,128)(2,1)S(1)}, bf16[1,768,256]{2,1,0:T(8,128)(2,1)S(1)}, bf16[1536,256]{1,0:T(8,128)(2,1)S(1)}, bf16[4,1536,128]{2,1,0:...) custom-call(s32[1,16]{1,0:T(1,128)S(1)} %copy-done.33, ...), custom_call_target="tpu_custom_call" | custom-call | tf_op jit(solution)/shard_map/pallas_call | solution.py:43
  26.0 1.2 copy-done.13
  31.0 2.5 shard_map.230
  36.5 2.8 shard_map.231
  39.4 10.6 %shard_map.232 = (bf16[768,256]{1,0:T(8,128)(2,1)S(1)}, bf16[1,768,256]{2,1,0:T(8,128)(2,1)S(1)}, bf16[1536,256]{1,0:T(8,128)(2,1)S(1)}, bf16[4,1536,128]{2,1,0:T(8,128)(2,1)S(1)}) custom-call(s32[1,16]{1,0:T(1,128)S(1)} %copy-done.34, s32[1,16]{1,0:T(1,128)S(1)} %copy-done.35, bf16[4,1536,128]{2,1,0:T(8,128)(2,1)S(1)} %get-tuple-element.62.kx, ...), custom_call_target="tpu_custom_call" | custom-call | tf_op jit(solution)/shard_map/pallas_call | solution.py:43
  52.3 1.6 collective-permute-done.5.refs_3_
  55.6 31.0 %shard_map.233 = (f32[768,512]{1,0:T(8,128)}, f32[768,512]{1,0:T(8,128)}, f32[2,512]{1,0:T(2,128)}, f32[2,512]{1,0:T(2,128)}, bf16[1024,512]{1,0:T(8,128)(2,1)},...) custom-call(f32[3,512]{1,0:T(4,128)} %gain.5, ...), custom_call_target="tpu_custom_call" | custom-call | tf_op jit(solution)/shard_map/pallas_call | solution.py:43
  87.4 3.1 collective-permute-done.8.refs_1_
  91.3 33.9 %shard_map.234 = (bf16[768,256]{1,0:T(8,128)(2,1)}, bf16[1,768,256]{2,1,0:T(8,128)(2,1)}, bf16[2,512,256]{2,1,0:T(8,128)(2,1)}, f32[768,512]{1,0:T(8,128)}, bf16[1,768,512]{2,1,0:T(8,128)(2,1)}) custom-call(s32[1,16]{1,0:T(1,128)} %dec_ref.5, s32[1,16]{1,0:T(1,128)} %enc_ref.3, bf16[4,1536,128]{2,1,0:T(8,128)(2,1)} %copy-done.7, ...), custom_call_target="tpu_custom_call" | custom-call | tf_op jit(solution)/shard_map/pallas_call | solution.py:43
  125.7 1.7 add_convert_fusion.2
  128.4 3.4 shard_map.235
  132.7 1.4 add_convert_fusion.1
  135.7 1.3 add_convert_fusion
  137.7 28.2 %shard_map.236 = (bf16[3,512,256]{2,1,0:T(8,128)(2,1)}, f32[768,512]{1,0:T(8,128)}, bf16[1,768,512]{2,1,0:T(8,128)(2,1)}) custom-call(s32[1,16]{1,0:T(1,128)} %dec_ref.5, bf16[4,1536,128]{2,1,0:T(8,128)(2,1)} %copy-done.11, bf16[4,1536,128]{2,1,0:T(8,128)(2,1)} %copy-done.12, bf16[4,1536,128]{2,1,0:T(8,128)(2,1)} %copy-done.13, ...), custom_call_target="tpu_custom_call" | custom-call | tf_op jit(solution)/shard_map/pallas_call | solution.py:43
  166.6 52.8 %all-reduce = (f32[3,512]{1,0:T(4,128)}, f32[3,512]{1,0:T(4,128)}) all-reduce(f32[3,512]{1,0:T(4,128)S(1)} %get-tuple-element.115, f32[3,512]{1,0:T(4,128)S(1)} %get-tuple-element.116), channel_id=1, replica_groups=mesh['rows'=16,'heads'=2] {'rows','heads'}, use_global_device_ids=true, to_apply=%region_7.0 | all-reduce | flops 3072 | bytes 24576 | tf_op jit(solution)/shard_map/psum | solution.py:696
  219.5 1.4 convert_add_fusion
  221.9 1.6 add_add_fusion
  223.5 124.2 %all-reduce.4.cloned.1.call-done = (bf16[3,512,256]{2,1,0:T(8,128)(2,1)}, bf16[256,512]{1,0:T(8,128)(2,1)}, bf16[512,256]{1,0:T(8,128)(2,1)}, bf16[2,512,256]{2,...) async-done(((bf16[3,512,256]{2,1,0:T(8,128)(2,1)}, bf16[256,512]{1,0:T(8,128)(2,1)}, bf16[512,256]{1,0:T(8,128)(2,1)}, ...) | async-done | bytes 4194320 | tf_op jit(solution)/shard_map/psum | solution.py:683
  347.6 1.9 convert_element_type.78
  349.5 1.8 convert_element_type.82
  352.2 1.3 convert_element_type.74
  354.5 1.6 convert_element_type.91
  356.1 1.6 convert_element_type.95
  (149 shorter events, 22.4 us)
Async XLA Ops:
  7.2 340.5 %all-reduce.4.cloned.1.call-start = ((), (), s32[]{:S(2)}) async-start(), calls=%async_computation | async-start | bytes 8388608 | tf_op jit(solution)/shard_map/psum | solution.py:683
  28.1 2.9 collective-permute-start
  28.5 1.7 collective-permute-start.1
  28.6 2.4 collective-permute-start.2
  29.0 24.8 %collective-permute-start.6 = (bf16[512,1024]{1,0:T(8,128)(2,1)}, bf16[512,1024]{1,0:T(8,128)(2,1)S(1)}, u32[]{:S(2)}, u32[]{:S(2)}) collective-permute-start(bf16[512,1024]{1,0:T(8,128)(2,1)} %refs_4_.3), channel_id=1, source_target_pairs={{0,1},{1,0},{2,3},{3,2},{4,5},{5,4},{6,7},{7,6},{8,9},{9,8},{10,11... | collective-permute-start | bytes 3145736 | tf_op jit(solution)/shard_map/ppermute | solution.py:585
  29.1 24.7 %collective-permute-start.7 = (bf16[1024,512]{1,0:T(8,128)(2,1)}, bf16[1024,512]{1,0:T(8,128)(2,1)S(1)}, u32[]{:S(2)}, u32[]{:S(2)}) collective-permute-start(bf16[1024,512]{1,0:T(8,128)(2,1)} %refs_6_.2), channel_id=1, source_target_pairs={{0,1},{1,0},{2,3},{3,2},{4,5},{5,4},{6,7},{7,6},{8,9},{9,8},{10,11... | collective-permute-start | bytes 3145736 | tf_op jit(solution)/shard_map/ppermute | solution.py:585
  36.2 3.3 collective-permute-start.3
  51.7 2.1 collective-permute-start.4
  51.9 2.0 collective-permute-start.5
  86.6 46.1 %collective-permute-start.16 = (bf16[512,1024]{1,0:T(8,128)(2,1)}, bf16[512,1024]{1,0:T(8,128)(2,1)S(1)}, u32[]{:S(2)}, u32[]{:S(2)}) collective-permute-start(bf16[512,1024]{1,0:T(8,128)(2,1)} %bitcast.20), channel_id=1, source_target_pairs={{0,1},{1,0},{2,3},{3,2},{4,5},{5,4},{6,7},{7,6},{8,9},{9,8},{10,11... | collective-permute-start | bytes 3145736 | tf_op jit(solution)/shard_map/ppermute | solution.py:585
  86.8 3.6 collective-permute-start.8
  87.2 38.5 %collective-permute-start.15 = (bf16[256,512]{1,0:T(8,128)(2,1)}, bf16[256,512]{1,0:T(8,128)(2,1)}, u32[]{:S(2)}, u32[]{:S(2)}) collective-permute-start(bf16[256,512]{1,0:T(8,128)(2,1)} %bitcast.24), channel_id=1, source_target_pairs={{0,1},{1,0},{2,3},{3,2},{4,5},{5,4},{6,7},{7,6},{8,9},{9,8},{10,11... | collective-permute-start | bytes 786440 | tf_op jit(solution)/shard_map/ppermute | solution.py:585
  91.2 36.2 %copy-start.20 = (bf16[512,256]{1,0:T(8,128)(2,1)S(1)}, bf16[512,256]{1,0:T(8,128)(2,1)}, u32[]{:S(2)}) copy-start(bf16[512,256]{1,0:T(8,128)(2,1)} %copy-done.19) | copy-start | bytes 786436
  91.2 36.2 %copy-start.24 = (bf16[768,512]{1,0:T(8,128)(2,1)S(1)}, bf16[768,512]{1,0:T(8,128)(2,1)}, u32[]{:S(2)}) copy-start(bf16[768,512]{1,0:T(8,128)(2,1)} %copy-done.23) | copy-start | bytes 2359300
  91.2 36.2 %copy-start.28 = (f32[768,1]{1,0:T(8,128)S(1)}, f32[768,1]{1,0:T(8,128)}, u32[]{:S(2)}) copy-start(f32[768,1]{1,0:T(8,128)} %copy-done.27) | copy-start | bytes 9220
  91.3 36.2 %copy-start.31 = (f32[3,512]{1,0:T(4,128)S(1)}, f32[3,512]{1,0:T(4,128)}, u32[]{:S(2)}) copy-start(f32[3,512]{1,0:T(4,128)} %gain.5) | copy-start | bytes 18436
  125.1 2.3 collective-permute-start.9
  125.3 10.3 %collective-permute-start.17 = (bf16[1024,512]{1,0:T(8,128)(2,1)}, bf16[1024,512]{1,0:T(8,128)(2,1)S(1)}, u32[]{:S(2)}, u32[]{:S(2)}) collective-permute-start(bf16[1024,512]{1,0:T(8,128)(2,1)} %bitcast.19), channel_id=1, source_target_pairs={{0,1},{1,0},{2,3},{3,2},{4,5},{5,4},{6,7},{7,6},{8,9},{9,8},{10,11... | collective-permute-start | bytes 3145736 | tf_op jit(solution)/shard_map/ppermute | solution.py:585
  131.9 2.1 collective-permute-start.13
  132.2 2.7 collective-permute-start.14
  132.5 4.4 %collective-permute-start.10 = (bf16[768,256]{1,0:T(8,128)(2,1)S(1)}, bf16[768,256]{1,0:T(8,128)(2,1)S(1)}, u32[]{:S(2)}, u32[]{:S(2)}) collective-permute-start(bf16[768,256]{1,0:T(8,128)(2,1)S(1)} %bitcast.13), channel_id=1, source_target_pairs={{0,1},{1,0},{2,3},{3,2},{4,5},{5,4},{6,7},{7,6},{8,9},{9,8},{10,11... | collective-permute-start | bytes 1179656 | tf_op jit(solution)/shard_map/ppermute | solution.py:585
  165.9 53.6 %copy-start.36 = (f32[768,512]{1,0:T(8,128)S(1)}, f32[768,512]{1,0:T(8,128)}, u32[]{:S(2)}) copy-start(f32[768,512]{1,0:T(8,128)} %get-tuple-element.88) | copy-start | bytes 4718596
  165.9 53.5 %collective-permute-start.12 = (bf16[768,512]{1,0:T(8,128)(2,1)}, bf16[768,512]{1,0:T(8,128)(2,1)S(1)}, u32[]{:S(2)}, u32[]{:S(2)}) collective-permute-start(bf16[768,512]{1,0:T(8,128)(2,1)} %bitcast.7), channel_id=1, source_target_pairs={{0,1},{1,0},{2,3},{3,2},{4,5},{5,4},{6,7},{7,6},{8,9},{9,8},{10,11... | collective-permute-start | bytes 2359304 | tf_op jit(solution)/shard_map/ppermute | solution.py:585
  166.3 54.5 %collective-permute-start.11 = (bf16[768,512]{1,0:T(8,128)(2,1)}, bf16[768,512]{1,0:T(8,128)(2,1)S(1)}, u32[]{:S(2)}, u32[]{:S(2)}) collective-permute-start(bf16[768,512]{1,0:T(8,128)(2,1)} %bitcast.21), channel_id=1, source_target_pairs={{0,1},{1,0},{2,3},{3,2},{4,5},{5,4},{6,7},{7,6},{8,9},{9,8},{10,11... | collective-permute-start | bytes 2359304 | tf_op jit(solution)/shard_map/ppermute | solution.py:585
  (50 other events, 357.4 us)
Sparse Core Ops, SparseCore 0:
  166.0 181.5 all-reduce.3
where the time goes:
time: 367 us; the launch traced here: 365 us
  waiting for transfers between devices  130 us (35%)
  Pallas kernels  128 us (35%)
  blocking collectives  52.8 us (14%)
  other arithmetic  18.9 us (5%)
  local copies, waits for them, and re-layouts  15.1 us (4%)
  between operations  14.7 us (4%)
  starting transfers between devices  4.98 us (1%)
    pallas_call x8, Pallas kernels, call(): pl.pallas_call(kernel, out_shape=outs, in_specs=[SMEM] * smem + [VMEM] *...  128 us
    psum x1, waiting for transfers between devices, over_rows(): return lax.psum(value.astype(BF16), 'rows').astype(F32)  124 us
    psum x1, blocking collectives, body(): lax.psum(jnp.concatenate([gains_low, gains_high]), ('rows', 'heads'))  52.8 us
    convert_element_type x12, other arithmetic, over_rows(): return lax.psum(value.astype(BF16), 'rows').astype(F32)  16 us
    unnamed x110, local copies, waits for them, and re-layouts  15.1 us
  transfers between devices with their start and end apart: 19, of which 5 were waited for; matrix products, arithmetic and copies ran while one was open for 2% of the time, Pallas kernels for 15%

commit v1 on v0

--- a/solution.py
+++ b/solution.py
@@ -554,6 +554,250 @@
 
     lax.fori_loop(0, length // SPAN, step, 0)
     split_out(wide, in_keep, in_send, in_keep.shape[0])
+
+
+LINK_RATE = 0.088
+HOP_TIME = 2.0
+
+
+def transfer_plan(orders, ready, sizes, bits):
+    steps = 2 * bits
+    busy = {}
+    left = {p: 0 for p in range(len(orders))}
+    at = {p: ready[p] for p in range(len(orders))}
+    plan, flying, clock = [], [], 0.0
+
+    def bit_of(p, step):
+        return orders[p][step] if step < bits else orders[p][steps - 1 - step]
+
+    def cost(p, step):
+        depth = step if step < bits else steps - 1 - step
+        amount = sizes[p] / 2 ** (depth + 1) * 2 / LINK_RATE
+        bit = bit_of(p, step)
+        if bit == bits - 1 and bits == 4:
+            return {3: 2 * amount, 2: amount}
+        return {bit: amount}
+
+    def rest(p):
+        return sum(max(cost(p, s).values()) + HOP_TIME for s in range(left[p], steps))
+
+    waiting = set(range(len(orders)))
+    while waiting or flying:
+        chosen = None
+        for p in sorted(waiting, key=lambda p: (-rest(p), p)):
+            need = cost(p, left[p])
+            if at[p] <= clock and all(busy.get(b, 0.0) <= clock + 1.0 for b in need):
+                chosen = p
+                break
+        if chosen is not None:
+            need = cost(chosen, left[chosen])
+            done = clock
+            for b, amount in need.items():
+                busy[b] = max(busy.get(b, 0.0), clock) + amount
+                done = max(done, busy[b])
+            plan.append(("send", chosen, left[chosen]))
+            flying.append((done + HOP_TIME, chosen))
+            waiting.discard(chosen)
+            continue
+        times = [t for t, _ in flying]
+        times += [at[p] for p in waiting if at[p] > clock]
+        times += [t - 1.0 for t in busy.values() if t - 1.0 > clock and waiting]
+        clock = max(clock, min(times))
+        for t, p in sorted(flying):
+            if t <= clock:
+                flying.remove((t, p))
+                plan.append(("take", p, left[p]))
+                left[p] += 1
+                at[p] = clock
+                if left[p] < steps:
+                    waiting.add(p)
+    return plan
+
+
+def rows_sum_kernel(table, bits, *refs):
+    count = len(table)
+    sources = max(max(e[0], -1 if e[1] is None else e[1]) for e in table) + 1
+    arrays, small, outs = refs[:sources], refs[sources], refs[sources + 1 : sources + 1 + table[-1][7] + 1]
+    small_out = refs[sources + 1 + len(outs)]
+    rest = list(refs[sources + 2 + len(outs) :])
+    take = lambda number: [rest.pop(0) for _ in range(number)]
+    held, mate, landing, final = take(count), take(count), take(count), take(count)
+    small_land, load_sem, mate_sem, send_sem, land_sem, store_sem, small_send, small_sem = rest
+    steps = 2 * bits
+    me = lax.axis_index("rows")
+    core = lax.axis_index("heads")
+
+    def partner(bit):
+        return {"rows": me + (1 << bit) - 2 * (me & (1 << bit)), "heads": core}
+
+    peers = [partner(bit) for bit in range(bits)] + [{"rows": me, "heads": 1 - core}]
+    barrier = pltpu.get_barrier_semaphore()
+    loads = []
+    for p, (source, pair, row, col, rows, cols, _, _) in enumerate(table):
+        window = (pl.ds(row, rows), pl.ds(col, cols))
+        pieces = [pltpu.make_async_copy(arrays[source].at[window], held[p], load_sem.at[p])]
+        if pair is not None:
+            pieces.append(pltpu.make_async_copy(arrays[pair].at[window], mate[p], mate_sem.at[p]))
+        for piece in pieces:
+            piece.start()
+        loads.append(pieces)
+    for peer in peers:
+        pl.semaphore_signal(barrier, inc=1, device_id=peer, device_id_type=pl.DeviceIdType.MESH)
+    pl.semaphore_wait(barrier, len(peers))
+
+    def remote(source, dest, send, land, peer):
+        copy = pltpu.make_async_remote_copy(
+            src_ref=source, dst_ref=dest, send_sem=send, recv_sem=land,
+            device_id=peer, device_id_type=pl.DeviceIdType.MESH,
+        )
+        copy.start()
+        return copy
+
+    def add(dest, rows, left, right, left_rows, right_rows):
+        total = left[left_rows, :].astype(F32) + right[right_rows, :].astype(F32)
+        dest[rows, :] = total.astype(BF16)
+
+    small_out[...] = small[...]
+    offset = [jnp.int32(0)] * count
+    copies = {}
+    stores = []
+    small_step = 0
+    small_copy = None
+    plan = transfer_plan(
+        [e[6] for e in table], [0.0] * count, [e[4] * e[5] * 2e-6 for e in table], bits
+    )
+    for number, (kind, p, step) in enumerate(plan):
+        _, _, row, col, rows, cols, order, out = table[p]
+        depth = step if step < bits else steps - 1 - step
+        bit = order[depth]
+        size = rows >> (depth + 1)
+        side = lax.shift_right_logical(me, bit) & 1
+        if kind == "send" and step < bits:
+            if step == 0:
+                for piece in loads[p]:
+                    piece.wait()
+                if len(loads[p]) == 2:
+                    add(held[p], slice(None), held[p], mate[p], slice(None), slice(None))
+            away = pl.ds(pl.multiple_of(offset[p] + (1 - side) * size, 16), size)
+            spot = pl.ds(rows - 2 * size, size)
+            copies[p] = remote(
+                held[p].at[away, :], landing[p].at[spot, :],
+                send_sem.at[p, step], land_sem.at[p, step], peers[bit],
+            )
+        elif kind == "send":
+            mine = pl.ds(pl.multiple_of(offset[p], 16), size)
+            copies[p] = remote(
+                final[p].at[mine, :], final[p].at[mine, :],
+                send_sem.at[p, step], land_sem.at[p, step], peers[bit],
+            )
+        elif step < bits:
+            copies[p].wait()
+            offset[p] = offset[p] + side * size
+            mine = pl.ds(pl.multiple_of(offset[p], 16), size)
+            spot = pl.ds(rows - 2 * size, size)
+            add(final[p] if step == bits - 1 else held[p], mine, held[p], landing[p], mine, spot)
+        else:
+            copies[p].wait()
+            offset[p] = offset[p] - side * size
+            if step == steps - 1:
+                window = (pl.ds(row, rows), pl.ds(col, cols))
+                store = pltpu.make_async_copy(final[p], outs[out].at[window], store_sem.at[p])
+                store.start()
+                stores.append(store)
+        if number % 4 == 0 and small_step <= len(peers):
+            if small_copy is not None:
+                small_copy.wait()
+                small_out[...] += small_land[small_step - 1]
+            if small_step < len(peers):
+                small_copy = remote(
+                    small_out, small_land.at[small_step], small_send.at[small_step],
+                    small_sem.at[small_step], peers[small_step],
+                )
+            small_step += 1
+    for store in stores:
+        store.wait()
+
+
+def widen_kernel(table, *refs):
+    outs = table[-1][7] + 1
+    arrays, dests = refs[:outs], refs[outs : 2 * outs]
+    rest = list(refs[2 * outs :])
+    low = [rest.pop(0) for _ in table]
+    wide = [rest.pop(0) for _ in table]
+    load_sem, store_sem = rest
+    loads, stores = [], []
+    for p, (_, _, row, col, rows, cols, _, out) in enumerate(table):
+        window = (pl.ds(row, rows), pl.ds(col, cols))
+        loads.append(pltpu.make_async_copy(arrays[out].at[window], low[p], load_sem.at[p]))
+        stores.append(pltpu.make_async_copy(wide[p], dests[out].at[window], store_sem.at[p]))
+        loads[p].start()
+    for p in range(len(table)):
+        loads[p].wait()
+        wide[p][...] = low[p][...].astype(F32)
+        stores[p].start()
+    for store in stores:
+        store.wait()
+
+
+def sum_over_rows(pairs, small):
+    size = lax.axis_size("rows")
+    bits = size.bit_length() - 1
+    arrays, table = [], []
+    for out, (own, other) in enumerate(pairs):
+        source = len(arrays)
+        arrays.append(own)
+        pair = None
+        if other is not None:
+            pair = source + 1
+            arrays.append(other)
+        rows, cols = own.shape
+        high, broad = (256, 512) if cols == 512 else (512, 256)
+        for row in range(0, rows, high):
+            for col in range(0, cols, broad):
+                table.append([source, pair, row, col, high, broad, None, out])
+    x_first, y_first = (0, 1, 2, 3), (1, 0, 2, 3)
+    z_first, z_other = (2, 0, 1, 3), (2, 1, 0, 3)
+    cycle = [x_first, y_first, z_first, x_first, y_first, z_other]
+    for p, entry in enumerate(table):
+        entry[6] = cycle[p % len(cycle)]
+    count = len(table)
+    buffers = [pltpu.VMEM((e[4], e[5]), BF16) for e in table]
+    small_shape = small.shape
+    sums = pl.pallas_call(
+        functools.partial(rows_sum_kernel, table, bits),
+        out_shape=[shape_of(own.shape, BF16) for own, _ in pairs] + [shape_of(small_shape, F32)],
+        in_specs=[pl.BlockSpec(memory_space=pl.ANY)] * len(arrays) + [VMEM],
+        out_specs=[pl.BlockSpec(memory_space=pl.ANY)] * len(pairs) + [VMEM],
+        scratch_shapes=buffers * 4
+        + [pltpu.VMEM((bits + 1, *small_shape), F32)]
+        + [pltpu.SemaphoreType.DMA((count,))] * 2
+        + [pltpu.SemaphoreType.DMA((count, 2 * bits))] * 2
+        + [pltpu.SemaphoreType.DMA((count,))]
+        + [pltpu.SemaphoreType.DMA((bits + 1,))] * 2,
+        compiler_params=pltpu.CompilerParams(
+            vmem_limit_bytes=40 * 2**20, collective_id=0, has_side_effects=True
+        ),
+    )(*arrays, small)
+    wide = pl.pallas_call(
+        functools.partial(widen_kernel, table),
+        out_shape=[shape_of(own.shape, F32) for own, _ in pairs],
+        in_specs=[pl.BlockSpec(memory_space=pl.ANY)] * len(pairs),
+        out_specs=[pl.BlockSpec(memory_space=pl.ANY)] * len(pairs),
+        scratch_shapes=buffers
+        + [pltpu.VMEM((e[4], e[5]), F32) for e in table]
+        + [pltpu.SemaphoreType.DMA((count,))] * 2,
+        compiler_params=pltpu.CompilerParams(vmem_limit_bytes=40 * 2**20),
+    )(*sums[:-1])
+    return [*wide, sums[-1]]
+
+
+def fits_kernel(pairs):
+    fits = all(
+        own.shape[1] == 512 and own.shape[0] % 256 == 0
+        or own.shape[1] % 256 == 0 and own.shape[0] % 512 == 0
+        for own, _ in pairs
+    )
+    return fits and lax.axis_size("rows") == 16 and lax.axis_size("heads") == 2
 
 
 def body(
@@ -679,22 +923,39 @@
     )
     input_grad = grad_base + collect(in_keep, in_send)
 
-    def over_rows(value):
-        return lax.psum(value.astype(BF16), "rows").astype(F32)
-
+    small = jnp.concatenate(
+        [gains_low, gains_high, biases_low, biases_high, jnp.zeros((2, width), F32)]
+    )
+    halves = [
+        (g_ffn_out, g_ffn_out_send),
+        (g_ffn_in, g_ffn_in_send),
+        (g_cross_out, g_cross_out_send),
+        (g_cross_q, g_cross_q_send),
+        (g_cross_kv.reshape(2 * width, local), None),
+        (g_self_out, g_self_out_send),
+        (g_self_qkv.reshape(3 * width, local), None),
+    ]
+    if fits_kernel(halves):
+        pairs = [(own, None if away is None else shift(away[0], 1)) for own, away in halves]
+        sums = sum_over_rows(pairs, small)
+    else:
+        totals = [own if away is None else collect(own, away) for own, away in halves]
+        sums = [lax.psum(total.astype(BF16), "rows").astype(F32) for total in totals]
+        sums.append(lax.psum(small, ("rows", "heads")))
+    s_ffn_out, s_ffn_in, s_cross_out, s_cross_q, s_cross_kv, s_self_out, s_self_qkv, sums_small = sums
     return (
         layer_out,
         input_grad,
         enc_grad,
-        over_rows(g_self_qkv),
-        over_rows(collect(g_self_out, g_self_out_send)),
-        over_rows(collect(g_cross_q, g_cross_q_send)),
-        over_rows(g_cross_kv),
-        over_rows(collect(g_cross_out, g_cross_out_send)),
-        over_rows(collect(g_ffn_in, g_ffn_in_send)),
-        over_rows(collect(g_ffn_out, g_ffn_out_send)),
-        lax.psum(jnp.concatenate([gains_low, gains_high]), ("rows", "heads")),
-        lax.psum(jnp.concatenate([biases_low, biases_high]), ("rows", "heads")),
+        s_self_qkv.reshape(3, width, local),
+        s_self_out,
+        s_cross_q,
+        s_cross_kv.reshape(2, width, local),
+        s_cross_out,
+        s_ffn_in,
+        s_ffn_out,
+        sums_small[:3],
+        sums_small[3:6],
     )
 
 

time: 367 us -> 271 us (0.74)
  waiting for transfers between devices: 130 us -> 6.13 us
  Pallas kernels: 128 us -> 225 us
  blocking collectives: 52.8 us -> 0 us
  other arithmetic: 18.9 us -> 5.33 us
  between operations: 14.7 us -> 1.51 us
  local copies, waits for them, and re-layouts: 15.1 us -> 23.1 us
    psum x1 -> x0, waiting for transfers between devices: 124 us -> none  [over_rows(): return lax.psum(value.astype(BF16), 'rows').astype(F32)]
    pallas_call x0 -> x2, Pallas kernels: none -> 93.8 us  [the longest x1 89.9 us: sum_over_rows(): pl.pallas_call(functools.partial(rows_sum_kernel, table, bits), out_shape...]
    psum x1 -> x0, blocking collectives: 52.8 us -> none  [body(): lax.psum(jnp.concatenate([gains_low, gains_high]), ('rows', 'heads'))]
    convert_element_type x12 -> x0, other arithmetic: 16 us -> none  [over_rows(): return lax.psum(value.astype(BF16), 'rows').astype(F32)]
    unnamed x110 -> x124, local copies, waits for them, and re-layouts: 15.1 us -> 22.5 us
  transfers between devices with their start and end apart: 19 -> 18, of which waited for: 5 -> 6; matrix products, arithmetic and copies ran while one was open for 2% -> 1% of each run, Pallas kernels for 15% -> 54%
where the time goes in v1:
time: 271 us; the launch traced here: 266 us
  Pallas kernels  225 us (83%)
  local copies, waits for them, and re-layouts  23.1 us (9%)
  waiting for transfers between devices  6.13 us (2%)
  other arithmetic  5.33 us (2%)
  starting transfers between devices  4.51 us (2%)
    pallas_call x8, Pallas kernels, call(): pl.pallas_call(kernel, out_shape=outs, in_specs=[SMEM] * smem + [VMEM] *...  131 us
    pallas_call x1, Pallas kernels, sum_over_rows(): pl.pallas_call(functools.partial(rows_sum_kernel, table, bits), out_shape...  89.9 us
    unnamed x124, local copies, waits for them, and re-layouts  22.5 us
    ppermute x18, waiting for transfers between devices, shift(): lax.ppermute(value, 'heads', [(d, (d + k) % parts) for d in range(parts)])  6.13 us
  transfers between devices with their start and end apart: 18, of which 6 were waited for; matrix products, arithmetic and copies ran while one was open for 1% of the time, Pallas kernels for 54%

profile of v1, /device:TPU:0, one launch (start us, length us, event | category | flops | bytes accessed | tf_op | source)
XLA Modules:
  0.0 265.7 jit_solution(6398566759130390373)
XLA Ops:
  0.7 1.4 copy-done
  2.1 1.1 copy-done.5
  3.9 16.1 %shard_map.229 = (bf16[768,256]{1,0:T(8,128)(2,1)S(1)}, bf16[1,768,256]{2,1,0:T(8,128)(2,1)S(1)}, bf16[1536,256]{1,0:T(8,128)(2,1)S(1)}, bf16[4,1536,128]{2,1,0:...) custom-call(s32[1,16]{1,0:T(1,128)S(1)} %copy-done.48, ...), custom_call_target="tpu_custom_call" | custom-call | tf_op jit(solution)/shard_map/pallas_call | solution.py:43
  19.9 1.2 copy-done.11
  25.0 2.5 shard_map.230
  27.5 1.1 copy-done.12
  30.5 2.8 %shard_map.231 = (bf16[4,1536,128]{2,1,0:T(8,128)(2,1)S(1)}, bf16[4,1536,128]{2,1,0:T(8,128)(2,1)S(1)}) custom-call(s32[1,16]{1,0:T(1,128)S(1)} %copy-done.50, bf16[1536,512]{1,0:T(8,128)(2,1)S(1)} %copy-done.2, bf16[2,512,256]{2,1,0:T(8,128)(2,1)S(1)} %copy-done.6), custom_call_target="tpu_custom_call" | custom-call | tf_op jit(solution)/shard_map/pallas_call | solution.py:43
  33.4 10.4 %shard_map.232 = (bf16[768,256]{1,0:T(8,128)(2,1)S(1)}, bf16[1,768,256]{2,1,0:T(8,128)(2,1)S(1)}, bf16[1536,256]{1,0:T(8,128)(2,1)S(1)}, bf16[4,1536,128]{2,1,0:T(8,128)(2,1)S(1)}) custom-call(s32[1,16]{1,0:T(1,128)S(1)} %copy-done.49, s32[1,16]{1,0:T(1,128)S(1)} %copy-done.50, bf16[4,1536,128]{2,1,0:T(8,128)(2,1)S(1)} %get-tuple-element.77.kx, ...), custom_call_target="tpu_custom_call" | custom-call | tf_op jit(solution)/shard_map/pallas_call | solution.py:43
  45.1 1.6 collective-permute-done.5.refs_3_
  46.8 1.0 copy-done.53
  48.5 31.0 %shard_map.233 = (f32[768,512]{1,0:T(8,128)}, f32[768,512]{1,0:T(8,128)}, f32[2,512]{1,0:T(2,128)}, f32[2,512]{1,0:T(2,128)}, bf16[1024,512]{1,0:T(8,128)(2,1)},...) custom-call(f32[3,512]{1,0:T(4,128)} %gain.5, ...), custom_call_target="tpu_custom_call" | custom-call | tf_op jit(solution)/shard_map/pallas_call | solution.py:43
  79.7 1.8 collective-permute-done.8.refs_1_
  82.3 35.2 %shard_map.234 = (bf16[768,256]{1,0:T(8,128)(2,1)}, bf16[1,768,256]{2,1,0:T(8,128)(2,1)}, bf16[2,512,256]{2,1,0:T(8,128)(2,1)}, f32[768,512]{1,0:T(8,128)}, bf16[1,768,512]{2,1,0:T(8,128)(2,1)}) custom-call(s32[1,16]{1,0:T(1,128)} %dec_ref.5, s32[1,16]{1,0:T(1,128)} %enc_ref.3, bf16[4,1536,128]{2,1,0:T(8,128)(2,1)} %copy-done.7, ...), custom_call_target="tpu_custom_call" | custom-call | tf_op jit(solution)/shard_map/pallas_call | solution.py:43
  119.6 1.0 copy-done.35
  120.5 4.2 %shard_map.235 = (f32[768,512]{1,0:T(8,128)S(1)}, f32[1,512]{1,0:T(1,128)S(1)}, f32[1,512]{1,0:T(1,128)S(1)}, bf16[512,256]{1,0:T(8,128)(2,1)S(1)}, bf16[1,512,2...) custom-call(f32[3,512]{1,0:T(4,128)S(1)} %copy-done.46, ...), custom_call_target="tpu_custom_call" | custom-call | tf_op jit(solution)/shard_map/pallas_call | solution.py:43
  129.4 29.1 %shard_map.236 = (bf16[3,512,256]{2,1,0:T(8,128)(2,1)}, f32[768,512]{1,0:T(8,128)}, bf16[1,768,512]{2,1,0:T(8,128)(2,1)}) custom-call(s32[1,16]{1,0:T(1,128)} %dec_ref.5, bf16[4,1536,128]{2,1,0:T(8,128)(2,1)} %copy-done.9, bf16[4,1536,128]{2,1,0:T(8,128)(2,1)} %copy-done.10, bf16[4,1536,128]{2,1,0:T(8,128)(2,1)} %copy-done.11, bf16[1536,256]{1,0:T(8,128)(2,1)} %copy-done.25, ...), custom_call_target="tpu_custom_call" | custom-call | tf_op jit(solution)/shard_map/pallas_call | solution.py:43
  159.4 1.2 copy-done.16
  160.6 1.1 copy-done.27
  162.7 0.9 copy-done.40
  163.6 0.9 copy-done.42
  165.5 89.9 %shard_map.237 = (bf16[1024,512]{1,0:T(8,128)(2,1)S(1)}, bf16[512,1024]{1,0:T(8,128)(2,1)S(1)}, bf16[256,512]{1,0:T(8,128)(2,1)S(1)}, bf16[512,256]{1,0:T(8,128)...) custom-call(bf16[1024,512]{1,0:T(8,128)(2,1)S(1)} %copy-done.15, ...), custom_call_target="tpu_custom_call" | custom-call | tf_op jit(solution)/shard_map/pallas_call | solution.py:766
  255.4 4.0 %shard_map.238 = (f32[1024,512]{1,0:T(8,128)}, f32[512,1024]{1,0:T(8,128)}, f32[256,512]{1,0:T(8,128)}, f32[512,256]{1,0:T(8,128)}, f32[1024,256]{1,0:T(8,128)},...) custom-call(bf16[1024,512]{1,0:T(8,128)(2,1)S(1)} %get-tuple-element.121.refs_0_, ...), custom_call_target="tpu_custom_call" | custom-call | tf_op jit(solution)/shard_map/pallas_call | solution.py:781
  260.0 2.6 convert_add_fusion
  262.6 2.7 %add_add_fusion = f32[768,512]{1,0:T(8,128)} fusion(f32[768,512]{1,0:T(8,128)S(1)} %get-tuple-element.94, f32[768,512]{1,0:T(8,128)S(1)} %copy-done.52, bf16[768,512]{1,0:T(8,128)(2,1)} %collective-permute-done.11), kind=kLoop, calls=%fused_computation.1 | loop fusion | flops 1179648 | bytes 5505024 | tf_op jit(solution)/shard_map/add | solution.py:924
  (151 shorter events, 19.4 us)
Async XLA Ops:
  22.0 2.9 %collective-permute-start = (bf16[768,256]{1,0:T(8,128)(2,1)S(1)}, bf16[768,256]{1,0:T(8,128)(2,1)S(1)}, u32[]{:S(2)}, u32[]{:S(2)}) collective-permute-start(bf16[768,256]{1,0:T(8,128)(2,1)S(1)} %bitcast.20), channel_id=1, source_target_pairs={{0,1},{1,0},{2,3},{3,2},{4,5},{5,4},{6,7},{7,6},{8,9},{9,8},{10,11... | collective-permute-start | bytes 1179656 | tf_op jit(solution)/shard_map/ppermute | solution.py:829
  22.5 1.7 collective-permute-start.1
  22.5 2.4 collective-permute-start.2
  23.0 23.7 %collective-permute-start.6 = (bf16[512,1024]{1,0:T(8,128)(2,1)}, bf16[512,1024]{1,0:T(8,128)(2,1)S(1)}, u32[]{:S(2)}, u32[]{:S(2)}) collective-permute-start(bf16[512,1024]{1,0:T(8,128)(2,1)} %refs_4_.3), channel_id=1, source_target_pairs={{0,1},{1,0},{2,3},{3,2},{4,5},{5,4},{6,7},{7,6},{8,9},{9,8},{10,11... | collective-permute-start | bytes 3145736 | tf_op jit(solution)/shard_map/ppermute | solution.py:829
  23.1 23.7 %collective-permute-start.7 = (bf16[1024,512]{1,0:T(8,128)(2,1)}, bf16[1024,512]{1,0:T(8,128)(2,1)S(1)}, u32[]{:S(2)}, u32[]{:S(2)}) collective-permute-start(bf16[1024,512]{1,0:T(8,128)(2,1)} %refs_6_.2), channel_id=1, source_target_pairs={{0,1},{1,0},{2,3},{3,2},{4,5},{5,4},{6,7},{7,6},{8,9},{9,8},{10,11... | collective-permute-start | bytes 3145736 | tf_op jit(solution)/shard_map/ppermute | solution.py:829
  30.1 3.2 %collective-permute-start.3 = (bf16[768,256]{1,0:T(8,128)(2,1)S(1)}, bf16[768,256]{1,0:T(8,128)(2,1)S(1)}, u32[]{:S(2)}, u32[]{:S(2)}) collective-permute-start(bf16[768,256]{1,0:T(8,128)(2,1)S(1)} %bitcast.22), channel_id=1, source_target_pairs={{0,1},{1,0},{2,3},{3,2},{4,5},{5,4},{6,7},{7,6},{8,9},{9,8},{10,11... | collective-permute-start | bytes 1179656 | tf_op jit(solution)/shard_map/ppermute | solution.py:829
  44.6 2.1 collective-permute-start.4
  44.8 2.0 collective-permute-start.5
  79.5 2.0 collective-permute-start.8
  82.2 37.2 %copy-start.20 = (bf16[512,256]{1,0:T(8,128)(2,1)S(1)}, bf16[512,256]{1,0:T(8,128)(2,1)}, u32[]{:S(2)}) copy-start(bf16[512,256]{1,0:T(8,128)(2,1)} %refs_2_.5) | copy-start | bytes 786436
  82.2 37.3 %copy-start.22 = (bf16[256,512]{1,0:T(8,128)(2,1)S(1)}, bf16[256,512]{1,0:T(8,128)(2,1)}, u32[]{:S(2)}) copy-start(bf16[256,512]{1,0:T(8,128)(2,1)} %copy-done.21) | copy-start | bytes 786436
  82.3 37.3 %copy-start.24 = (bf16[512,256]{1,0:T(8,128)(2,1)S(1)}, bf16[512,256]{1,0:T(8,128)(2,1)}, u32[]{:S(2)}) copy-start(bf16[512,256]{1,0:T(8,128)(2,1)} %copy-done.23) | copy-start | bytes 786436
  82.3 37.3 %copy-start.29 = (bf16[768,512]{1,0:T(8,128)(2,1)S(1)}, bf16[768,512]{1,0:T(8,128)(2,1)}, u32[]{:S(2)}) copy-start(bf16[768,512]{1,0:T(8,128)(2,1)} %copy-done.28) | copy-start | bytes 2359300
  82.3 37.3 %copy-start.34 = (f32[768,1]{1,0:T(8,128)S(1)}, f32[768,1]{1,0:T(8,128)}, u32[]{:S(2)}) copy-start(f32[768,1]{1,0:T(8,128)} %copy-done.33) | copy-start | bytes 9220
  82.3 37.3 %copy-start.46 = (f32[3,512]{1,0:T(4,128)S(1)}, f32[3,512]{1,0:T(4,128)}, u32[]{:S(2)}) copy-start(f32[3,512]{1,0:T(4,128)} %gain.5) | copy-start | bytes 18436
  117.5 1.9 collective-permute-start.9
  117.7 41.6 %collective-permute-start.13 = (bf16[1024,512]{1,0:T(8,128)(2,1)}, bf16[1024,512]{1,0:T(8,128)(2,1)}, u32[]{:S(2)}, u32[]{:S(2)}) collective-permute-start(bf16[1024,512]{1,0:T(8,128)(2,1)} %bitcast.8), channel_id=1, source_target_pairs={{0,1},{1,0},{2,3},{3,2},{4,5},{5,4},{6,7},{7,6},{8,9},{9,8},{10,11... | collective-permute-start | bytes 3145736 | tf_op jit(solution)/shard_map/ppermute | solution.py:829
  118.1 41.3 %collective-permute-start.14 = (bf16[512,1024]{1,0:T(8,128)(2,1)}, bf16[512,1024]{1,0:T(8,128)(2,1)}, u32[]{:S(2)}, u32[]{:S(2)}) collective-permute-start(bf16[512,1024]{1,0:T(8,128)(2,1)} %bitcast.9), channel_id=1, source_target_pairs={{0,1},{1,0},{2,3},{3,2},{4,5},{5,4},{6,7},{7,6},{8,9},{9,8},{10,11... | collective-permute-start | bytes 3145736 | tf_op jit(solution)/shard_map/ppermute | solution.py:829
  118.2 9.2 %collective-permute-start.15 = (bf16[256,512]{1,0:T(8,128)(2,1)}, bf16[256,512]{1,0:T(8,128)(2,1)S(1)}, u32[]{:S(2)}, u32[]{:S(2)}) collective-permute-start(bf16[256,512]{1,0:T(8,128)(2,1)} %bitcast.10), channel_id=1, source_target_pairs={{0,1},{1,0},{2,3},{3,2},{4,5},{5,4},{6,7},{7,6},{8,9},{9,8},{10,11... | collective-permute-start | bytes 786440 | tf_op jit(solution)/shard_map/ppermute | solution.py:829
  126.9 1.7 collective-permute-start.10
  127.0 133.0 %collective-permute-start.12 = (bf16[768,512]{1,0:T(8,128)(2,1)}, bf16[768,512]{1,0:T(8,128)(2,1)}, u32[]{:S(2)}, u32[]{:S(2)}) collective-permute-start(bf16[768,512]{1,0:T(8,128)(2,1)} %bitcast.7), channel_id=1, source_target_pairs={{0,1},{1,0},{2,3},{3,2},{4,5},{5,4},{6,7},{7,6},{8,9},{9,8},{10,11... | collective-permute-start | bytes 2359304 | tf_op jit(solution)/shard_map/ppermute | solution.py:829
  128.1 30.3 %collective-permute-start.16 = (bf16[512,256]{1,0:T(8,128)(2,1)}, bf16[512,256]{1,0:T(8,128)(2,1)S(1)}, u32[]{:S(2)}, u32[]{:S(2)}) collective-permute-start(bf16[512,256]{1,0:T(8,128)(2,1)} %bitcast.11), channel_id=1, source_target_pairs={{0,1},{1,0},{2,3},{3,2},{4,5},{5,4},{6,7},{7,6},{8,9},{9,8},{10,11... | collective-permute-start | bytes 786440 | tf_op jit(solution)/shard_map/ppermute | solution.py:829
  128.6 30.7 %collective-permute-start.17 = (bf16[256,512]{1,0:T(8,128)(2,1)}, bf16[256,512]{1,0:T(8,128)(2,1)}, u32[]{:S(2)}, u32[]{:S(2)}) collective-permute-start(bf16[256,512]{1,0:T(8,128)(2,1)} %bitcast.13), channel_id=1, source_target_pairs={{0,1},{1,0},{2,3},{3,2},{4,5},{5,4},{6,7},{7,6},{8,9},{9,8},{10,11... | collective-permute-start | bytes 786440 | tf_op jit(solution)/shard_map/ppermute | solution.py:829
  159.1 103.5 %collective-permute-start.11 = (bf16[768,512]{1,0:T(8,128)(2,1)}, bf16[768,512]{1,0:T(8,128)(2,1)}, u32[]{:S(2)}, u32[]{:S(2)}) collective-permute-start(bf16[768,512]{1,0:T(8,128)(2,1)} %bitcast.25), channel_id=1, source_target_pairs={{0,1},{1,0},{2,3},{3,2},{4,5},{5,4},{6,7},{7,6},{8,9},{9,8},{10,11... | collective-permute-start | bytes 2359304 | tf_op jit(solution)/shard_map/ppermute | solution.py:829
  (56 other events, 548.1 us)
